TPU v7x, 256 devices: a whole 4x4x8 slice. The times are simulated.
256 devices in a mesh: clip: 4 (over z_lo), seg: 64 (over x, y, z_hi, core).
Axes of the slice: x: 4, y: 4, z: 8 (z_hi: 2, z_lo: 4; z = z_hi * 4 + z_lo), core: 2. Of those that a mesh axis runs over, the one named last changes fastest.
Arguments:
- spectra: bfloat16 [16, 2, 1024, 1536], P('clip', None, 'seg'), may hold values from -6 to 6
- target: bfloat16 [16, 786432], P('clip', 'seg'), may hold values from -12 to 12
- lengths: int32 [16], P('clip'), may hold values from 768 to 1536, as said below
Outputs:
- loss: float32 [], replicated
- spec_grad: bfloat16 [16, 2, 1024, 1536], P('clip', None, 'seg')
Inputs may be any that keep to these rules, and one draw needn't show every extreme that they name: `lengths`: some clip has all 1536 frames.
All inputs are finite; a program needn't handle non-finite values.
Results may differ from a plain program's by a relative error of at most 0.0092.
Values may be sent and summed in bfloat16 or wider, within the bound.
A program may use at most 128 MiB of HBM per device.

v0:
```python
from functools import partial
import math
import jax
import jax.numpy as jnp
from jax import lax
from jax.sharding import Mesh
from jax.sharding import PartitionSpec as P

BINS = 1024
NFFT = 2048
HOP = 512
SEG = ("seg_0", "seg_1", "seg_2", "seg_3")
EPS_MAG = 0.1
EPS_RATIO = 1e-05


def shifted(block, axis, distance):
    devices = range(lax.axis_size(axis))
    route = [(i - distance, i) for i in devices if i - distance in devices]
    return lax.ppermute(block, axis, route)


def over_axes(x, axes):
    for axis in axes:
        x = lax.psum(x, axis)
    return x


def from_everyone(x, axis):
    devices = lax.axis_size(axis)
    return lax.all_to_all(jnp.broadcast_to(x[None], (devices, *x.shape)), axis, 0, 0, tiled=True)


def of_everyone(x, axis):
    return from_everyone(x, axis).sum(axis=0)


def wave_table(bins_index, time_index, points, factor):
    halfway = points // 2
    is_sine = bins_index >= halfway
    harmonic = jnp.where(is_sine, bins_index - halfway, bins_index)
    angles = (harmonic * time_index % points).astype(jnp.float32) * (2.0 * math.pi / points)
    window = 0.5 - 0.5 * jnp.cos(time_index.astype(jnp.float32) * (2.0 * math.pi / points))
    entry_value = jnp.where(is_sine, -jnp.sin(angles), jnp.cos(angles))
    return (entry_value * window * factor).astype(jnp.bfloat16)


def analysis_rows(points, anchor, height):
    time_index = anchor + jnp.arange(height, dtype=jnp.int32)
    return wave_table(
        jnp.arange(points, dtype=jnp.int32)[None, :],
        time_index[:, None],
        points,
        1.0 / math.sqrt(points),
    )


def analysis_cols(points, anchor, height):
    bins_index = anchor + jnp.arange(height, dtype=jnp.int32)
    return wave_table(
        bins_index[:, None],
        jnp.arange(points, dtype=jnp.int32)[None, :],
        points,
        1.0 / math.sqrt(points),
    )


def synth_rows(anchor, height):
    bins_index = anchor + jnp.arange(height, dtype=jnp.int32)
    return wave_table(
        bins_index[:, None], jnp.arange(NFFT, dtype=jnp.int32)[None, :], NFFT, 1.0 / math.sqrt(BINS)
    )


def synth_cols(anchor, height):
    time_index = anchor + jnp.arange(height, dtype=jnp.int32)
    return wave_table(
        jnp.arange(2 * BINS, dtype=jnp.int32)[None, :],
        time_index[:, None],
        NFFT,
        1.0 / math.sqrt(BINS),
    )


def blocked_product(operand, along, make_rows, pattern, out_shape):
    length_in = operand.shape[along]
    stride = min(512, length_in)

    def turn(turn_index, summed):
        anchor = turn_index * stride
        portion = lax.dynamic_slice_in_dim(operand, anchor, stride, along)
        return summed + jnp.einsum(
            pattern, portion, make_rows(anchor, stride), preferred_element_type=jnp.float32
        )

    return lax.fori_loop(0, length_in // stride, turn, jnp.zeros(out_shape, jnp.float32))


def spread_parts(quarters):
    return sum(
        (
            jnp.pad(quarters[:, :, quarter], ((0, 0), (quarter, 3 - quarter), (0, 0)))
            for quarter in range(4)
        )
    )


def framed(signal, beyond, stride):
    frame_count = signal.shape[1] // stride
    padded = jnp.concatenate([signal, beyond], axis=1).reshape(
        signal.shape[0], frame_count + 3, stride
    )
    return jnp.concatenate(
        [padded[:, quarter : quarter + frame_count] for quarter in range(4)], axis=2
    )


def body(spectra, target, lengths):
    clip_count = spectra.shape[0]
    frames_all = spectra.shape[3]
    samples = target.shape[1]
    rows_here = samples // HOP
    seg_index = lax.axis_index(SEG)
    start_sample = seg_index * samples
    block = lax.all_to_all(spectra, SEG, split_axis=3, concat_axis=2, tiled=True)
    stacked = block.reshape(block.shape[0], 2 * BINS, block.shape[3])
    signals = blocked_product(
        stacked, 1, synth_rows, "ckf,km->cfm", (block.shape[0], block.shape[3], NFFT)
    )
    spilled = spread_parts(signals.reshape(clip_count, rows_here, 4, HOP))
    spill = shifted(spilled[:, rows_here:], SEG, 1)
    estimate = (
        spilled[:, :rows_here] + jnp.pad(spill, ((0, 0), (0, rows_here - 3), (0, 0)))
    ).reshape(clip_count, samples)
    sample_index = start_sample + jnp.arange(samples, dtype=jnp.int32)
    inside = sample_index[None, :] < (lengths * HOP)[:, None]
    est_wave = jnp.where(inside, estimate, 0.0).astype(jnp.bfloat16)
    clean = jnp.where(inside, target, jnp.zeros_like(target))
    sizes_list = (NFFT // 4, NFFT // 2, NFFT)
    beyond_est, beyond_tgt = shifted((est_wave[:, : 3 * HOP], clean[:, : 3 * HOP]), SEG, -1)
    beyond_list = [
        (beyond_est[:, : 3 * (points // 4)], beyond_tgt[:, : 3 * (points // 4)])
        for points in sizes_list
    ]
    saved = []
    spread_list = []
    energy_list = []
    logterm_list = []
    for points, beyond_pair in zip(sizes_list, beyond_list):
        stride = points // 4
        halfway = points // 2
        frame_count = samples // stride
        paired = jnp.stack(
            [framed(est_wave, beyond_pair[0], stride), framed(clean, beyond_pair[1], stride)]
        )
        spectra_pair = blocked_product(
            paired,
            3,
            partial(analysis_rows, points),
            "ecfm,mj->ecfj",
            (2, clip_count, frame_count, points),
        )
        est_real = spectra_pair[0, :, :, :halfway]
        est_imag = spectra_pair[0, :, :, halfway:]
        tgt_real = spectra_pair[1, :, :, :halfway]
        tgt_imag = spectra_pair[1, :, :, halfway:]
        est_mag = jnp.sqrt(est_real * est_real + est_imag * est_imag + EPS_MAG)
        tgt_mag = jnp.sqrt(tgt_real * tgt_real + tgt_imag * tgt_imag + EPS_MAG)
        usable_count = lengths * (HOP // stride)
        frame_index = start_sample // stride + jnp.arange(frame_count, dtype=jnp.int32)
        usable = frame_index[None, :, None] < usable_count[:, None, None]
        mag_gap = est_mag - tgt_mag
        log_gap = jnp.log(est_mag) - jnp.log(tgt_mag)
        entries = (usable_count * halfway).astype(jnp.float32)
        spread_list.append(jnp.sum(jnp.where(usable, mag_gap * mag_gap, 0.0), axis=(1, 2)))
        energy_list.append(jnp.sum(jnp.where(usable, tgt_mag * tgt_mag, 0.0), axis=(1, 2)))
        logterm_list.append(
            jnp.sum(jnp.where(usable, log_gap * log_gap, 0.0), axis=(1, 2)) / entries
        )
        saved.append((est_real, est_imag, est_mag, mag_gap, log_gap, usable, entries))
    spreads = jnp.stack(spread_list)
    energies = jnp.stack(energy_list)
    logterms = jnp.stack(logterm_list)
    spreads, energies, logterms = (
        over_axes(spreads, SEG),
        over_axes(energies, SEG),
        over_axes(logterms, SEG),
    )
    own_loss = jnp.sum(jnp.sqrt((spreads + EPS_RATIO) / energies) + logterms)
    loss = of_everyone(own_loss, "clip") / (3 * clip_count * lax.axis_size("clip"))
    ratio_weight = 1.0 / jnp.sqrt((spreads + EPS_RATIO) * energies)
    gradient = jnp.zeros((clip_count, samples), jnp.float32)
    extras = []
    for level, points in enumerate(sizes_list):
        stride = points // 4
        frame_count = samples // stride
        est_real, est_imag, est_mag, mag_gap, log_gap, usable, entries = saved[level]
        grad_mag = jnp.where(
            usable,
            mag_gap * ratio_weight[level][:, None, None]
            + 2.0 * log_gap / (est_mag * entries[:, None, None]),
            0.0,
        ) * (frames_all * BINS)
        grad_x = jnp.concatenate(
            [grad_mag * est_real / est_mag, grad_mag * est_imag / est_mag], axis=2
        ).astype(jnp.bfloat16)
        grad_frames = blocked_product(
            grad_x,
            2,
            partial(analysis_cols, points),
            "cfj,jm->cfm",
            (clip_count, frame_count, points),
        )
        spread_back = spread_parts(grad_frames.reshape(clip_count, frame_count, 4, stride))
        gradient = gradient + spread_back[:, :frame_count].reshape(clip_count, samples)
        extras.append(spread_back[:, frame_count:].reshape(clip_count, 3 * stride))
    joined = sum(
        (jnp.pad(portion, ((0, 0), (0, 3 * HOP - portion.shape[1]))) for portion in extras)
    )
    received = shifted(joined, SEG, 1)
    gradient = gradient + jnp.pad(received, ((0, 0), (0, samples - 3 * HOP)))
    grad_wave = jnp.where(inside, gradient, 0.0).astype(jnp.bfloat16)
    grad_hops = grad_wave.reshape(clip_count, rows_here, HOP)
    following = shifted(grad_hops[:, :3], SEG, -1)
    extended = jnp.concatenate([grad_hops, following], axis=1)
    grad_signals = jnp.concatenate(
        [extended[:, quarter : quarter + rows_here] for quarter in range(4)], axis=2
    )
    grad_time = blocked_product(
        grad_signals, 2, synth_cols, "cfm,mk->ckf", (clip_count, 2 * BINS, rows_here)
    )
    rounded = grad_time.reshape(clip_count, 2, BINS, rows_here).astype(jnp.bfloat16)
    spec_grad = lax.all_to_all(rounded, SEG, split_axis=2, concat_axis=3, tiled=True)
    return (loss, spec_grad)


def solution(mesh):
    finer = Mesh(
        mesh.devices.reshape(mesh.shape["clip"], 4, 4, 2, 2),
        ("clip", "seg_0", "seg_1", "seg_2", "seg_3"),
    )
    placed = (P("clip", None, SEG, None), P("clip", SEG), P("clip"))
    return jax.shard_map(
        body,
        mesh=finer,
        in_specs=placed,
        out_specs=(P(), P("clip", None, SEG, None)),
        check_vma=False,
    )
```

profile of v0, /device:TPU:33, one launch (start us, length us, event | category | flops | bytes accessed | tf_op | source)
XLA Modules:
  0.0 549.3 jit_solution(1532712928770241731)
XLA Ops:
  54.4 70.7 %while.106 = (s32[]{:T(128)}, f32[4,24,2048]{2,1,0:T(8,128)S(1)}, bf16[4,2048,24]{1,2,0:T(8,128)(2,1)S(1)}, s32[]{:T(128)}, s32[]{:T(128)}, /*index=5*/s32[]{:T(128)}, s32[]{:T(128)}) while((s32[]{:T(128)}, f32[4,24,2048]{2,1,0:T(8,128)S(1)}, bf16[4,2048,24]{1,2,0:T(8,128)(2,1)S(1)}, s32[]{:T(128)}, s32[]{:T(128)}, ...), condition=%wide.region_1.2_spmd.clone, body=%wide.region_0.1_spmd.clone.sunk | while | flops 221654016 | bytes 1692817 | solution.py:96
  54.7 17.4 %convolution_add_fusion.8 = f32[4,24,2048]{2,1,0:T(8,128)S(1)} fusion(f32[2048]{0:T(1024)S(1)} %multiply_subtract_fusion.13, s32[512]{0:T(512)S(1)} %add_select_fusion.21, pred[512]{0:T(512)(128)(4,1)S(1)} %fusion.240, f32[4,24,2048]{2,1,0:T(8,128)S(1)} %get-tuple-element.896, pred[]{:T(512)S(6)} %compare.52, ...), kind=kOutput, calls=%fused_computation.10.clone.1 | convolution fusion | flops 221642752 | bytes 1681925 | tf_op jit(solution)/shard_map/while/body/eval_jaxpr/ckf,km->cfm/dot_general | solution.py:92
  72.2 17.4 %convolution_add_fusion.8 = f32[4,24,2048]{2,1,0:T(8,128)S(1)} fusion(f32[2048]{0:T(1024)S(1)} %multiply_subtract_fusion.13, s32[512]{0:T(512)S(1)} %add_select_fusion.21, pred[512]{0:T(512)(128)(4,1)S(1)} %fusion.240, f32[4,24,2048]{2,1,0:T(8,128)S(1)} %get-tuple-element.896, pred[]{:T(512)S(6)} %compare.52, ...), kind=kOutput, calls=%fused_computation.10.clone.1 | convolution fusion | flops 221642752 | bytes 1681925 | tf_op jit(solution)/shard_map/while/body/eval_jaxpr/ckf,km->cfm/dot_general | solution.py:92
  89.8 17.4 %convolution_add_fusion.8 = f32[4,24,2048]{2,1,0:T(8,128)S(1)} fusion(f32[2048]{0:T(1024)S(1)} %multiply_subtract_fusion.13, s32[512]{0:T(512)S(1)} %add_select_fusion.21, pred[512]{0:T(512)(128)(4,1)S(1)} %fusion.240, f32[4,24,2048]{2,1,0:T(8,128)S(1)} %get-tuple-element.896, pred[]{:T(512)S(6)} %compare.52, ...), kind=kOutput, calls=%fused_computation.10.clone.1 | convolution fusion | flops 221642752 | bytes 1681925 | tf_op jit(solution)/shard_map/while/body/eval_jaxpr/ckf,km->cfm/dot_general | solution.py:92
  107.3 17.4 %convolution_add_fusion.8 = f32[4,24,2048]{2,1,0:T(8,128)S(1)} fusion(f32[2048]{0:T(1024)S(1)} %multiply_subtract_fusion.13, s32[512]{0:T(512)S(1)} %add_select_fusion.21, pred[512]{0:T(512)(128)(4,1)S(1)} %fusion.240, f32[4,24,2048]{2,1,0:T(8,128)S(1)} %get-tuple-element.896, pred[]{:T(512)S(6)} %compare.52, ...), kind=kOutput, calls=%fused_computation.10.clone.1 | convolution fusion | flops 221642752 | bytes 1681925 | tf_op jit(solution)/shard_map/while/body/eval_jaxpr/ckf,km->cfm/dot_general | solution.py:92
  145.8 74.5 %while.108 = (s32[]{:T(128)}, f32[2,4,24,2048]{3,2,1,0:T(8,128)S(1)}, bf16[2,4,24,2048]{3,2,1,0:T(8,128)(2,1)}, s32[]{:T(128)}, s32[]{:T(128)}, /*index=5*/s32[]{:T(128)}, s32[]{:T(128)}) while((s32[]{:T(128)}, f32[2,4,24,2048]{3,2,1,0:T(8,128)S(1)}, bf16[2,4,24,2048]{3,2,1,0:T(8,128)(2,1)}, s32[]{:T(128)}, s32[]{:T(128)}, ...), condition=%wide.region_7.8_spmd.clone, body=%wide.region_6.7_spmd.clone.sunk | while | flops 423373824 | bytes 3371153 | solution.py:96
  146.1 18.4 %convolution_add_fusion.9 = f32[2,4,24,2048]{3,2,1,0:T(8,128)S(1)} fusion(f32[512]{0:T(512)S(1)} %multiply_subtract_fusion.15, s32[512]{0:T(512)S(1)} %iota_add_fusion.14, s32[2048]{0:T(1024)S(1)} %add_select_fusion.23, pred[2048]{0:T(1024)(128)(4,1)S(1)} %iota_compare_fusion.8, f32[2,4,24,2048]{3,2,1,0:T(8,128)S(1)} %get-tuple-element.938, ...), kind=kOutput, calls=%fused_computation.69.clone.1 | convolution fusion | flops 423362560 | bytes 3356677 | tf_op jit(solution)/shard_map/while/body/eval_jaxpr/ecfm,mj->ecfj/dot_general | solution.py:92
  164.6 18.4 %convolution_add_fusion.9 = f32[2,4,24,2048]{3,2,1,0:T(8,128)S(1)} fusion(f32[512]{0:T(512)S(1)} %multiply_subtract_fusion.15, s32[512]{0:T(512)S(1)} %iota_add_fusion.14, s32[2048]{0:T(1024)S(1)} %add_select_fusion.23, pred[2048]{0:T(1024)(128)(4,1)S(1)} %iota_compare_fusion.8, f32[2,4,24,2048]{3,2,1,0:T(8,128)S(1)} %get-tuple-element.938, ...), kind=kOutput, calls=%fused_computation.69.clone.1 | convolution fusion | flops 423362560 | bytes 3356677 | tf_op jit(solution)/shard_map/while/body/eval_jaxpr/ecfm,mj->ecfj/dot_general | solution.py:92
  183.1 18.4 %convolution_add_fusion.9 = f32[2,4,24,2048]{3,2,1,0:T(8,128)S(1)} fusion(f32[512]{0:T(512)S(1)} %multiply_subtract_fusion.15, s32[512]{0:T(512)S(1)} %iota_add_fusion.14, s32[2048]{0:T(1024)S(1)} %add_select_fusion.23, pred[2048]{0:T(1024)(128)(4,1)S(1)} %iota_compare_fusion.8, f32[2,4,24,2048]{3,2,1,0:T(8,128)S(1)} %get-tuple-element.938, ...), kind=kOutput, calls=%fused_computation.69.clone.1 | convolution fusion | flops 423362560 | bytes 3356677 | tf_op jit(solution)/shard_map/while/body/eval_jaxpr/ecfm,mj->ecfj/dot_general | solution.py:92
  201.6 18.4 %convolution_add_fusion.9 = f32[2,4,24,2048]{3,2,1,0:T(8,128)S(1)} fusion(f32[512]{0:T(512)S(1)} %multiply_subtract_fusion.15, s32[512]{0:T(512)S(1)} %iota_add_fusion.14, s32[2048]{0:T(1024)S(1)} %add_select_fusion.23, pred[2048]{0:T(1024)(128)(4,1)S(1)} %iota_compare_fusion.8, f32[2,4,24,2048]{3,2,1,0:T(8,128)S(1)} %get-tuple-element.938, ...), kind=kOutput, calls=%fused_computation.69.clone.1 | convolution fusion | flops 423362560 | bytes 3356677 | tf_op jit(solution)/shard_map/while/body/eval_jaxpr/ecfm,mj->ecfj/dot_general | solution.py:92
  227.3 20.9 %while.107 = (s32[]{:T(128)}, f32[2,4,48,1024]{3,2,1,0:T(8,128)S(1)}, bf16[2,4,48,1024]{3,2,1,0:T(8,128)(2,1)}, s32[]{:T(128)}, s32[]{:T(128)}, /*index=5*/s32[]{:T(128)}, s32[]{:T(128)}) while((s32[]{:T(128)}, f32[2,4,48,1024]{3,2,1,0:T(8,128)S(1)}, bf16[2,4,48,1024]{3,2,1,0:T(8,128)(2,1)}, s32[]{:T(128)}, s32[]{:T(128)}, ...), condition=%wide.region_4.5_spmd.clone, body=%wide.region_3.4_spmd.clone.sunk | while | flops 413408256 | bytes 3557521 | solution.py:96
  259.8 15.9 %all-reduce.21 = (f32[3,4]{1,0:T(4,128)}, f32[3,4]{1,0:T(4,128)}, f32[3,4]{1,0:T(4,128)}) all-reduce(f32[3,4]{1,0:T(4,128)S(1)} %pad_maximum_fusion.13, f32[3,4]{1,0:T(4,128)S(1)} %pad_maximum_fusion.12, f32[3,4]{1,0:T(4,128)S(1)} %pad_maximum_fusion.11), channel_id=1, replica_groups=mesh['clip'=4,'seg_0'=4,'seg_1'=4,'seg_2'=2,'seg_3'=2] {'seg_0'}, use_global_device_ids=true, to_apply=%region_23.24 | all-reduce | flops 36 | bytes 288 | tf_op jit(solution)/shard_map/psum | solution.py:25
  297.4 20.8 %while.109 = (s32[]{:T(128)}, f32[4,48,1024]{2,1,0:T(8,128)}, bf16[4,48,1024]{2,1,0:T(8,128)(2,1)S(1)}, s32[]{:T(128)}, s32[]{:T(128)}, /*index=5*/s32[]{:T(128)}, s32[]{:T(128)}) while((s32[]{:T(128)}, f32[4,48,1024]{2,1,0:T(8,128)}, bf16[4,48,1024]{2,1,0:T(8,128)(2,1)S(1)}, s32[]{:T(128)}, s32[]{:T(128)}, ...), condition=%wide.region_30.31_spmd.clone, body=%wide.region_29.30_spmd.clone.sunk | while | flops 211688448 | bytes 1782929 | solution.py:96
  325.4 77.4 %while.110 = (s32[]{:T(128)}, f32[4,24,2048]{2,1,0:T(8,128)}, bf16[4,24,2048]{2,1,0:T(8,128)(2,1)S(1)}, s32[]{:T(128)}, s32[]{:T(128)}, /*index=5*/s32[]{:T(128)}, s32[]{:T(128)}) while((s32[]{:T(128)}, f32[4,24,2048]{2,1,0:T(8,128)}, bf16[4,24,2048]{2,1,0:T(8,128)(2,1)S(1)}, s32[]{:T(128)}, s32[]{:T(128)}, ...), condition=%wide.region_32.33_spmd.clone, body=%wide.region_31.32_spmd.clone.sunk | while | flops 221654016 | bytes 1692817 | solution.py:96
  325.7 18.3 %convolution_add_fusion.11 = f32[4,24,2048]{2,1,0:T(8,128)} fusion(f32[2048]{0:T(1024)S(1)} %multiply_subtract_fusion.17, s32[512]{0:T(512)S(1)} %add_select_fusion.25, pred[512]{0:T(512)(128)(4,1)S(1)} %fusion.250, f32[4,24,2048]{2,1,0:T(8,128)} %get-tuple-element.959, pred[]{:T(512)S(6)} %compare.56, ...), kind=kOutput, calls=%fused_computation.130.clone.1 | convolution fusion | flops 221642752 | bytes 1681925 | tf_op jit(solution)/shard_map/while/body/eval_jaxpr/cfj,jm->cfm/dot_general | solution.py:92
  344.1 19.4 %convolution_add_fusion.11 = f32[4,24,2048]{2,1,0:T(8,128)} fusion(f32[2048]{0:T(1024)S(1)} %multiply_subtract_fusion.17, s32[512]{0:T(512)S(1)} %add_select_fusion.25, pred[512]{0:T(512)(128)(4,1)S(1)} %fusion.250, f32[4,24,2048]{2,1,0:T(8,128)} %get-tuple-element.959, pred[]{:T(512)S(6)} %compare.56, ...), kind=kOutput, calls=%fused_computation.130.clone.1 | convolution fusion | flops 221642752 | bytes 1681925 | tf_op jit(solution)/shard_map/while/body/eval_jaxpr/cfj,jm->cfm/dot_general | solution.py:92
  363.6 19.4 %convolution_add_fusion.11 = f32[4,24,2048]{2,1,0:T(8,128)} fusion(f32[2048]{0:T(1024)S(1)} %multiply_subtract_fusion.17, s32[512]{0:T(512)S(1)} %add_select_fusion.25, pred[512]{0:T(512)(128)(4,1)S(1)} %fusion.250, f32[4,24,2048]{2,1,0:T(8,128)} %get-tuple-element.959, pred[]{:T(512)S(6)} %compare.56, ...), kind=kOutput, calls=%fused_computation.130.clone.1 | convolution fusion | flops 221642752 | bytes 1681925 | tf_op jit(solution)/shard_map/while/body/eval_jaxpr/cfj,jm->cfm/dot_general | solution.py:92
  383.1 19.4 %convolution_add_fusion.11 = f32[4,24,2048]{2,1,0:T(8,128)} fusion(f32[2048]{0:T(1024)S(1)} %multiply_subtract_fusion.17, s32[512]{0:T(512)S(1)} %add_select_fusion.25, pred[512]{0:T(512)(128)(4,1)S(1)} %fusion.250, f32[4,24,2048]{2,1,0:T(8,128)} %get-tuple-element.959, pred[]{:T(512)S(6)} %compare.56, ...), kind=kOutput, calls=%fused_computation.130.clone.1 | convolution fusion | flops 221642752 | bytes 1681925 | tf_op jit(solution)/shard_map/while/body/eval_jaxpr/cfj,jm->cfm/dot_general | solution.py:92
  434.8 70.4 %while.111 = (s32[]{:T(128)}, f32[4,2048,24]{1,2,0:T(8,128)S(1)}, bf16[4,24,2048]{2,1,0:T(8,128)(2,1)S(1)}, s32[]{:T(128)}, s32[]{:T(128)}, /*index=5*/s32[]{:T(128)}, s32[]{:T(128)}) while((s32[]{:T(128)}, f32[4,2048,24]{1,2,0:T(8,128)S(1)}, bf16[4,24,2048]{2,1,0:T(8,128)(2,1)S(1)}, s32[]{:T(128)}, s32[]{:T(128)}, ...), condition=%wide.region_34.35_spmd.clone, body=%wide.region_33.34_spmd.clone.sunk | while | flops 221654016 | bytes 1699985 | solution.py:96
  435.1 17.4 %fusion.253 = f32[4,2048,24]{1,2,0:T(8,128)S(1)} fusion(f32[512]{0:T(512)S(1)} %multiply_subtract_fusion.18, s32[512]{0:T(512)S(1)} %iota_add_fusion.15, s32[2048]{0:T(1024)S(1)} %add_select_fusion.26, pred[2048]{0:T(1024)(128)(4,1)S(1)} %iota_compare_fusion.9, f32[4,2048,24]{1,2,0:T(8,128)S(1)} %get-tuple-element.1001, pred[]{:T(512)S(6)} %compare.57, ...), kind=kOutput, calls=%fused_computation.160.clone.1 | convolution fusion | flops 221642752 | bytes 1685509 | tf_op jit(solution)/shard_map/while/body/eval_jaxpr/cfm,mk->ckf/dot_general | solution.py:92
  452.6 17.4 %fusion.253 = f32[4,2048,24]{1,2,0:T(8,128)S(1)} fusion(f32[512]{0:T(512)S(1)} %multiply_subtract_fusion.18, s32[512]{0:T(512)S(1)} %iota_add_fusion.15, s32[2048]{0:T(1024)S(1)} %add_select_fusion.26, pred[2048]{0:T(1024)(128)(4,1)S(1)} %iota_compare_fusion.9, f32[4,2048,24]{1,2,0:T(8,128)S(1)} %get-tuple-element.1001, pred[]{:T(512)S(6)} %compare.57, ...), kind=kOutput, calls=%fused_computation.160.clone.1 | convolution fusion | flops 221642752 | bytes 1685509 | tf_op jit(solution)/shard_map/while/body/eval_jaxpr/cfm,mk->ckf/dot_general | solution.py:92
  470.1 17.4 %fusion.253 = f32[4,2048,24]{1,2,0:T(8,128)S(1)} fusion(f32[512]{0:T(512)S(1)} %multiply_subtract_fusion.18, s32[512]{0:T(512)S(1)} %iota_add_fusion.15, s32[2048]{0:T(1024)S(1)} %add_select_fusion.26, pred[2048]{0:T(1024)(128)(4,1)S(1)} %iota_compare_fusion.9, f32[4,2048,24]{1,2,0:T(8,128)S(1)} %get-tuple-element.1001, pred[]{:T(512)S(6)} %compare.57, ...), kind=kOutput, calls=%fused_computation.160.clone.1 | convolution fusion | flops 221642752 | bytes 1685509 | tf_op jit(solution)/shard_map/while/body/eval_jaxpr/cfm,mk->ckf/dot_general | solution.py:92
  487.6 17.4 %fusion.253 = f32[4,2048,24]{1,2,0:T(8,128)S(1)} fusion(f32[512]{0:T(512)S(1)} %multiply_subtract_fusion.18, s32[512]{0:T(512)S(1)} %iota_add_fusion.15, s32[2048]{0:T(1024)S(1)} %add_select_fusion.26, pred[2048]{0:T(1024)(128)(4,1)S(1)} %iota_compare_fusion.9, f32[4,2048,24]{1,2,0:T(8,128)S(1)} %get-tuple-element.1001, pred[]{:T(512)S(6)} %compare.57, ...), kind=kOutput, calls=%fused_computation.160.clone.1 | convolution fusion | flops 221642752 | bytes 1685509 | tf_op jit(solution)/shard_map/while/body/eval_jaxpr/cfm,mk->ckf/dot_general | solution.py:92
  519.5 18.3 %all-to-all-done.2 = bf16[64,2,1536]{2,1,0:T(2,128)(2,1)S(1)} async-done(((bf16[64,2,1536]{2,1,0:T(2,128)(2,1)}), bf16[64,2,1536]{2,1,0:T(2,128)(2,1)S(1)}, u32[]{:S(2)}, u32[]{:S(2)}) %all-to-all-start.2) | async-done | bytes 393248 | tf_op jit(solution)/shard_map/all_to_all | solution.py:233
  (281 shorter events, 219.0 us)
Async XLA Ops:
  0.6 23.0 %copy-start.19 = (s32[4]{0:T(128)S(1)}, s32[4]{0:T(128)}, u32[]{:S(2)}) copy-start(s32[4]{0:T(128)} %param.17) | copy-start | bytes 52
  8.6 33.4 %all-to-all-start = ((bf16[64,2,1536]{2,1,0:T(2,128)(2,1)}), bf16[64,2,1536]{2,1,0:T(2,128)(2,1)S(1)}, u32[]{:S(2)}, u32[]{:S(2)}) async-start(bf16[64,2,1536]{2,1,0:T(2,128)(2,1)} %reshape.462), calls=%async_computation | async-start | bytes 786432 | tf_op jit(solution)/shard_map/all_to_all | solution.py:125
  24.2 105.7 %copy-start.17 = (s32[4]{0:T(128)}, s32[4]{0:T(128)S(1)}, u32[]{:S(2)}) copy-start(s32[4]{0:T(128)S(1)} %get-tuple-element.765) | copy-start | bytes 52
  47.9 6.5 %copy-start.6 = (f32[4,24,2048]{2,1,0:T(8,128)S(1)}, f32[4,24,2048]{2,1,0:T(8,128)}, u32[]{:S(2)}) copy-start(f32[4,24,2048]{2,1,0:T(8,128)} %custom-call) | copy-start | bytes 2359300
  126.5 3.3 collective-permute-start
  130.1 9.5 %collective-permute-start.1 = (bf16[4,1536]{1,0:T(4,128)(2,1)S(1)}, bf16[4,1536]{1,0:T(4,128)(2,1)S(1)}, u32[]{:S(2)}, u32[]{:S(2)}) collective-permute-start(bf16[4,1536]{1,0:T(4,128)(2,1)S(1)} %slice.297), channel_id=1, source_target_pairs={{1,0},{2,1},{3,2},{4,3},{5,4},{6,5},{7,6},{8,7},{9,8},{10,9},{11,1... | collective-permute-start | bytes 36872 | tf_op jit(solution)/shard_map/ppermute | solution.py:20
  132.5 9.5 %collective-permute-start.2 = (bf16[4,1536]{1,0:T(4,128)(2,1)S(1)}, bf16[4,1536]{1,0:T(4,128)(2,1)S(1)}, u32[]{:S(2)}, u32[]{:S(2)}) collective-permute-start(bf16[4,1536]{1,0:T(4,128)(2,1)S(1)} %slice.303), channel_id=1, source_target_pairs={{1,0},{2,1},{3,2},{4,3},{5,4},{6,5},{7,6},{8,7},{9,8},{10,9},{11,1... | collective-permute-start | bytes 36872 | tf_op jit(solution)/shard_map/ppermute | solution.py:20
  139.6 80.8 %copy-start.14 = (bf16[4,1536]{1,0:T(4,128)(2,1)}, bf16[4,1536]{1,0:T(4,128)(2,1)S(1)}, u32[]{:S(2)}) copy-start(bf16[4,1536]{1,0:T(4,128)(2,1)S(1)} %collective-permute-done.1) | copy-start | bytes 36868
  220.4 29.0 %copy-start = (f32[2,4,24,2048]{3,2,1,0:T(8,128)}, f32[2,4,24,2048]{3,2,1,0:T(8,128)S(1)}, u32[]{:S(2)}) copy-start(f32[2,4,24,2048]{3,2,1,0:T(8,128)S(1)} %get-tuple-element.568) | copy-start | bytes 4718596
  227.3 20.9 %slice-start.1 = ((bf16[4,1536]{1,0:T(4,128)(2,1)}), bf16[4,384]{1,0:T(4,128)(2,1)S(1)}, s32[]{:S(2)}) async-start(bf16[4,1536]{1,0:T(4,128)(2,1)} %copy-done.14), calls=%async_computation.4 | async-start | bytes 6144 | tf_op jit(solution)/shard_map/slice | solution.py:142
  227.3 21.8 %slice-start.2 = ((bf16[4,1536]{1,0:T(4,128)(2,1)}), bf16[4,384]{1,0:T(4,128)(2,1)S(1)}, s32[]{:S(2)}) async-start(bf16[4,1536]{1,0:T(4,128)(2,1)} %copy-done.15), calls=%async_computation.5 | async-start | bytes 6144 | tf_op jit(solution)/shard_map/slice | solution.py:142
  249.2 4.3 copy-start.9
  253.6 4.7 copy-start.27
  253.6 6.1 %copy-start.20 = (s32[4]{0:T(128)S(1)}, s32[4]{0:T(128)}, u32[]{:S(2)}) copy-start(s32[4]{0:T(128)} %param.17) | copy-start | bytes 52
  253.7 42.1 %copy-start.16 = (f32[4]{0:T(128)S(1)}, f32[4]{0:T(128)}, u32[]{:S(2)}) copy-start(f32[4]{0:T(128)} %get-tuple-element.763) | copy-start | bytes 52
  318.1 6.7 %copy-start.1 = (f32[2,4,24,2048]{3,2,1,0:T(8,128)S(1)}, f32[2,4,24,2048]{3,2,1,0:T(8,128)}, u32[]{:S(2)}) copy-start(f32[2,4,24,2048]{3,2,1,0:T(8,128)} %copy-done) | copy-start | bytes 4718596
  412.0 13.6 %slice-start = ((f32[4,51,256]{2,0,1:T(4,128)}), f32[4,48,256]{2,0,1:T(4,128)S(1)}, s32[]{:S(2)}) async-start(f32[4,51,256]{2,0,1:T(4,128)} %pad_add_fusion.2), calls=%async_computation.3 | async-start | bytes 393216 | tf_op jit(solution)/shard_map/slice | solution.py:215
  412.0 13.6 %copy-start.8 = (s32[12288]{0:T(1024)S(1)}, s32[12288]{0:T(1024)}, u32[]{:S(2)}) copy-start(s32[12288]{0:T(1024)} %iota_add_fusion.6) | copy-start | bytes 147460
  412.0 13.5 %copy-start.18 = (s32[4]{0:T(128)S(1)}, s32[4]{0:T(128)}, u32[]{:S(2)}) copy-start(s32[4]{0:T(128)} %copy-done.17) | copy-start | bytes 52
  412.8 22.0 %copy-start.5 = (f32[4,2048,24]{1,2,0:T(8,128)S(1)}, f32[4,2048,24]{1,2,0:T(8,128)}, u32[]{:S(2)}) copy-start(f32[4,2048,24]{1,2,0:T(8,128)} %custom-call.5) | copy-start | bytes 2359300
  413.3 12.3 %collective-permute-start.3 = (f32[4,1536]{1,0:T(4,128)S(1)}, f32[4,1536]{1,0:T(4,128)S(1)}, u32[]{:S(2)}, u32[]{:S(2)}) collective-permute-start(f32[4,1536]{1,0:T(4,128)S(1)} %add_add_fusion.3), channel_id=1, source_target_pairs={{0,1},{1,2},{2,3},{3,4},{4,5},{5,6},{6,7},{7,8},{8,9},{9,10},{10,1... | collective-permute-start | bytes 73736 | tf_op jit(solution)/shard_map/ppermute | solution.py:20
  422.3 88.5 %all-to-all-start.1 = ((f32[4,1,1]{2,1,0:T(1,128)}), f32[4,1,1]{2,1,0:T(1,128)S(1)}, u32[]{:S(2)}, u32[]{:S(2)}) async-start(f32[4,1,1]{2,1,0:T(1,128)} %broadcast_in_dim.314), calls=%async_computation.1 | async-start | bytes 4096 | tf_op jit(solution)/shard_map/all_to_all | solution.py:31
  425.7 9.0 %collective-permute-start.4 = (bf16[4,3,512]{2,1,0:T(4,128)(2,1)S(1)}, bf16[4,3,512]{2,1,0:T(4,128)(2,1)S(1)}, u32[]{:S(2)}, u32[]{:S(2)}) collective-permute-start(bf16[4,3,512]{2,1,0:T(4,128)(2,1)S(1)} %slice.346), channel_id=1, source_target_pairs={{1,0},{2,1},{3,2},{4,3},{5,4},{6,5},{7,6},{8,7},{9,8},{10,9},{11,1... | collective-permute-start | bytes 36872 | tf_op jit(solution)/shard_map/ppermute | solution.py:20
  510.9 26.9 %all-to-all-start.2 = ((bf16[64,2,1536]{2,1,0:T(2,128)(2,1)}), bf16[64,2,1536]{2,1,0:T(2,128)(2,1)S(1)}, u32[]{:S(2)}, u32[]{:S(2)}) async-start(bf16[64,2,1536]{2,1,0:T(2,128)(2,1)} %reshape.464), calls=%async_computation.2 | async-start | bytes 786432 | tf_op jit(solution)/shard_map/all_to_all | solution.py:233
  (19 other events, 66.4 us)
where the time goes:
time: 557 us; the launch traced here: 549 us
  matrix products  340 us (61%)
  local copies, waits for them, and re-layouts  56.7 us (10%)
  waiting for transfers between devices  46.6 us (8%)
  starting transfers between devices  40.3 us (7%)
  blocking collectives  34.2 us (6%)
  other arithmetic  25 us (4%)
    dot_general x22, matrix products, turn(): jnp.einsum(pattern, portion, make_rows(anchor, stride), preferred_element...  340 us
    psum x4, blocking collectives, over_axes(): x = lax.psum(x, axis)  34.2 us
    unnamed x84, local copies, waits for them, and re-layouts  18.4 us
    all_to_all x1, waiting for transfers between devices, body(): lax.all_to_all(rounded, SEG, split_axis=2, concat_axis=3, tiled=True)  18.3 us
    ppermute x5, starting transfers between devices, shifted(): return lax.ppermute(block, axis, route)  15.8 us
    all_to_all x1, waiting for transfers between devices, body(): lax.all_to_all(spectra, SEG, split_axis=3, concat_axis=2, tiled=True)  15.3 us
    all_to_all x1, starting transfers between devices, body(): lax.all_to_all(spectra, SEG, split_axis=3, concat_axis=2, tiled=True)  13.9 us
    ppermute x5, waiting for transfers between devices, shifted(): return lax.ppermute(block, axis, route)  13 us
  transfers between devices with their start and end apart: 8, of which 5 were waited for; matrix products, arithmetic and copies ran while one was open for 15% of the time, Pallas kernels for 0%

commit v1 on v0

--- a/solution.py
+++ b/solution.py
@@ -22,7 +22,7 @@
 
 def over_axes(x, axes):
     for axis in axes:
-        x = lax.psum(x, axis)
+        x = jnp.sum(lax.all_gather(x, axis), axis=0)
     return x
 
 

time: 557 us -> 628 us (1.13)
  blocking collectives: 34.2 us -> 95.2 us
    all_gather x0 -> x12, blocking collectives: none -> 95.2 us  [over_axes(): x = jnp.sum(lax.all_gather(x, axis), axis=0)]
    psum x4 -> x0, blocking collectives: 34.2 us -> none  [over_axes(): x = lax.psum(x, axis)]
    unnamed x84 -> x80, local copies, waits for them, and re-layouts: 18.4 us -> 18.4 us
  transfers between devices with their start and end apart: 8 -> 8, of which waited for: 5 -> 6; matrix products, arithmetic and copies ran while one was open for 15% -> 14% of each run, Pallas kernels for 0% -> 0%
where the time goes in v1:
time: 628 us; the launch traced here: 620 us
  matrix products  341 us (54%)
  blocking collectives  95.2 us (15%)
  local copies, waits for them, and re-layouts  57.8 us (9%)
  waiting for transfers between devices  47.2 us (8%)
  starting transfers between devices  41.9 us (7%)
  other arithmetic  29.8 us (5%)
    dot_general x22, matrix products, turn(): jnp.einsum(pattern, portion, make_rows(anchor, stride), preferred_element...  341 us
    all_gather x12, blocking collectives, over_axes(): x = jnp.sum(lax.all_gather(x, axis), axis=0)  95.2 us
    unnamed x80, local copies, waits for them, and re-layouts  18.4 us
    all_to_all x1, waiting for transfers between devices, body(): lax.all_to_all(rounded, SEG, split_axis=2, concat_axis=3, tiled=True)  18.3 us
    all_to_all x1, waiting for transfers between devices, body(): lax.all_to_all(spectra, SEG, split_axis=3, concat_axis=2, tiled=True)  15.9 us
    ppermute x5, starting transfers between devices, shifted(): return lax.ppermute(block, axis, route)  15.7 us
    all_to_all x1, starting transfers between devices, body(): lax.all_to_all(spectra, SEG, split_axis=3, concat_axis=2, tiled=True)  13.9 us
    ppermute x5, waiting for transfers between devices, shifted(): return lax.ppermute(block, axis, route)  13 us
  transfers between devices with their start and end apart: 8, of which 6 were waited for; matrix products, arithmetic and copies ran while one was open for 14% of the time, Pallas kernels for 0%

profile of v1, /device:TPU:33, one launch (start us, length us, event | category | flops | bytes accessed | tf_op | source)
XLA Modules:
  0.0 620.3 jit_solution(5219433742629546422)
XLA Ops:
  26.1 15.9 %all-to-all-done = bf16[64,2,1536]{2,1,0:T(2,128)(2,1)S(1)} async-done(((bf16[64,2,1536]{2,1,0:T(2,128)(2,1)}), bf16[64,2,1536]{2,1,0:T(2,128)(2,1)S(1)}, u32[]{:S(2)}, u32[]{:S(2)}) %all-to-all-start) | async-done | bytes 393248 | tf_op jit(solution)/shard_map/all_to_all | solution.py:125
  54.4 70.7 %while.106 = (s32[]{:T(128)}, f32[4,24,2048]{2,1,0:T(8,128)S(1)}, bf16[4,2048,24]{1,2,0:T(8,128)(2,1)S(1)}, s32[]{:T(128)}, s32[]{:T(128)}, /*index=5*/s32[]{:T(128)}, s32[]{:T(128)}) while((s32[]{:T(128)}, f32[4,24,2048]{2,1,0:T(8,128)S(1)}, bf16[4,2048,24]{1,2,0:T(8,128)(2,1)S(1)}, s32[]{:T(128)}, s32[]{:T(128)}, ...), condition=%wide.region_1.2_spmd.clone, body=%wide.region_0.1_spmd.clone.sunk | while | flops 221654016 | bytes 1692817 | solution.py:96
  54.7 17.4 %convolution_add_fusion.8 = f32[4,24,2048]{2,1,0:T(8,128)S(1)} fusion(f32[2048]{0:T(1024)S(1)} %multiply_subtract_fusion.13, s32[512]{0:T(512)S(1)} %add_select_fusion.21, pred[512]{0:T(512)(128)(4,1)S(1)} %fusion.240, f32[4,24,2048]{2,1,0:T(8,128)S(1)} %get-tuple-element.884, pred[]{:T(512)S(6)} %compare.52, ...), kind=kOutput, calls=%fused_computation.10.clone.1 | convolution fusion | flops 221642752 | bytes 1681925 | tf_op jit(solution)/shard_map/while/body/eval_jaxpr/ckf,km->cfm/dot_general | solution.py:92
  72.2 17.4 %convolution_add_fusion.8 = f32[4,24,2048]{2,1,0:T(8,128)S(1)} fusion(f32[2048]{0:T(1024)S(1)} %multiply_subtract_fusion.13, s32[512]{0:T(512)S(1)} %add_select_fusion.21, pred[512]{0:T(512)(128)(4,1)S(1)} %fusion.240, f32[4,24,2048]{2,1,0:T(8,128)S(1)} %get-tuple-element.884, pred[]{:T(512)S(6)} %compare.52, ...), kind=kOutput, calls=%fused_computation.10.clone.1 | convolution fusion | flops 221642752 | bytes 1681925 | tf_op jit(solution)/shard_map/while/body/eval_jaxpr/ckf,km->cfm/dot_general | solution.py:92
  89.8 17.4 %convolution_add_fusion.8 = f32[4,24,2048]{2,1,0:T(8,128)S(1)} fusion(f32[2048]{0:T(1024)S(1)} %multiply_subtract_fusion.13, s32[512]{0:T(512)S(1)} %add_select_fusion.21, pred[512]{0:T(512)(128)(4,1)S(1)} %fusion.240, f32[4,24,2048]{2,1,0:T(8,128)S(1)} %get-tuple-element.884, pred[]{:T(512)S(6)} %compare.52, ...), kind=kOutput, calls=%fused_computation.10.clone.1 | convolution fusion | flops 221642752 | bytes 1681925 | tf_op jit(solution)/shard_map/while/body/eval_jaxpr/ckf,km->cfm/dot_general | solution.py:92
  107.3 17.4 %convolution_add_fusion.8 = f32[4,24,2048]{2,1,0:T(8,128)S(1)} fusion(f32[2048]{0:T(1024)S(1)} %multiply_subtract_fusion.13, s32[512]{0:T(512)S(1)} %add_select_fusion.21, pred[512]{0:T(512)(128)(4,1)S(1)} %fusion.240, f32[4,24,2048]{2,1,0:T(8,128)S(1)} %get-tuple-element.884, pred[]{:T(512)S(6)} %compare.52, ...), kind=kOutput, calls=%fused_computation.10.clone.1 | convolution fusion | flops 221642752 | bytes 1681925 | tf_op jit(solution)/shard_map/while/body/eval_jaxpr/ckf,km->cfm/dot_general | solution.py:92
  150.8 20.7 %while.107 = (s32[]{:T(128)}, f32[2,4,48,1024]{3,2,1,0:T(8,128)S(1)}, bf16[2,4,48,1024]{3,2,1,0:T(8,128)(2,1)}, s32[]{:T(128)}, s32[]{:T(128)}, /*index=5*/s32[]{:T(128)}, s32[]{:T(128)}) while((s32[]{:T(128)}, f32[2,4,48,1024]{3,2,1,0:T(8,128)S(1)}, bf16[2,4,48,1024]{3,2,1,0:T(8,128)(2,1)}, s32[]{:T(128)}, s32[]{:T(128)}, ...), condition=%wide.region_4.5_spmd.clone, body=%wide.region_3.4_spmd.clone.sunk | while | flops 413408256 | bytes 3557521 | solution.py:96
  176.3 74.5 %while.108 = (s32[]{:T(128)}, f32[2,4,24,2048]{3,2,1,0:T(8,128)S(1)}, bf16[2,4,24,2048]{3,2,1,0:T(8,128)(2,1)}, s32[]{:T(128)}, s32[]{:T(128)}, /*index=5*/s32[]{:T(128)}, s32[]{:T(128)}) while((s32[]{:T(128)}, f32[2,4,24,2048]{3,2,1,0:T(8,128)S(1)}, bf16[2,4,24,2048]{3,2,1,0:T(8,128)(2,1)}, s32[]{:T(128)}, s32[]{:T(128)}, ...), condition=%wide.region_7.8_spmd.clone, body=%wide.region_6.7_spmd.clone.sunk | while | flops 423373824 | bytes 3371153 | solution.py:96
  176.5 18.4 %convolution_add_fusion.9 = f32[2,4,24,2048]{3,2,1,0:T(8,128)S(1)} fusion(f32[512]{0:T(512)S(1)} %multiply_subtract_fusion.15, s32[512]{0:T(512)S(1)} %iota_add_fusion.14, s32[2048]{0:T(1024)S(1)} %add_select_fusion.23, pred[2048]{0:T(1024)(128)(4,1)S(1)} %iota_compare_fusion.8, f32[2,4,24,2048]{3,2,1,0:T(8,128)S(1)} %get-tuple-element.905, ...), kind=kOutput, calls=%fused_computation.69.clone.1 | convolution fusion | flops 423362560 | bytes 3356677 | tf_op jit(solution)/shard_map/while/body/eval_jaxpr/ecfm,mj->ecfj/dot_general | solution.py:92
  195.0 18.4 %convolution_add_fusion.9 = f32[2,4,24,2048]{3,2,1,0:T(8,128)S(1)} fusion(f32[512]{0:T(512)S(1)} %multiply_subtract_fusion.15, s32[512]{0:T(512)S(1)} %iota_add_fusion.14, s32[2048]{0:T(1024)S(1)} %add_select_fusion.23, pred[2048]{0:T(1024)(128)(4,1)S(1)} %iota_compare_fusion.8, f32[2,4,24,2048]{3,2,1,0:T(8,128)S(1)} %get-tuple-element.905, ...), kind=kOutput, calls=%fused_computation.69.clone.1 | convolution fusion | flops 423362560 | bytes 3356677 | tf_op jit(solution)/shard_map/while/body/eval_jaxpr/ecfm,mj->ecfj/dot_general | solution.py:92
  213.5 18.4 %convolution_add_fusion.9 = f32[2,4,24,2048]{3,2,1,0:T(8,128)S(1)} fusion(f32[512]{0:T(512)S(1)} %multiply_subtract_fusion.15, s32[512]{0:T(512)S(1)} %iota_add_fusion.14, s32[2048]{0:T(1024)S(1)} %add_select_fusion.23, pred[2048]{0:T(1024)(128)(4,1)S(1)} %iota_compare_fusion.8, f32[2,4,24,2048]{3,2,1,0:T(8,128)S(1)} %get-tuple-element.905, ...), kind=kOutput, calls=%fused_computation.69.clone.1 | convolution fusion | flops 423362560 | bytes 3356677 | tf_op jit(solution)/shard_map/while/body/eval_jaxpr/ecfm,mj->ecfj/dot_general | solution.py:92
  232.0 18.4 %convolution_add_fusion.9 = f32[2,4,24,2048]{3,2,1,0:T(8,128)S(1)} fusion(f32[512]{0:T(512)S(1)} %multiply_subtract_fusion.15, s32[512]{0:T(512)S(1)} %iota_add_fusion.14, s32[2048]{0:T(1024)S(1)} %add_select_fusion.23, pred[2048]{0:T(1024)(128)(4,1)S(1)} %iota_compare_fusion.8, f32[2,4,24,2048]{3,2,1,0:T(8,128)S(1)} %get-tuple-element.905, ...), kind=kOutput, calls=%fused_computation.69.clone.1 | convolution fusion | flops 423362560 | bytes 3356677 | tf_op jit(solution)/shard_map/while/body/eval_jaxpr/ecfm,mj->ecfj/dot_general | solution.py:92
  365.1 21.9 %while.109 = (s32[]{:T(128)}, f32[4,48,1024]{2,1,0:T(8,128)}, bf16[4,48,1024]{2,1,0:T(8,128)(2,1)}, s32[]{:T(128)}, s32[]{:T(128)}, /*index=5*/s32[]{:T(128)}, s32[]{:T(128)}) while((s32[]{:T(128)}, f32[4,48,1024]{2,1,0:T(8,128)}, bf16[4,48,1024]{2,1,0:T(8,128)(2,1)}, s32[]{:T(128)}, s32[]{:T(128)}, /*index=5*/s32[]{:T(128)}, ...), condition=%wide.region_30.31_spmd.clone, body=%wide.region_29.30_spmd.clone.sunk | while | flops 211688448 | bytes 1782929 | solution.py:96
  394.4 77.4 %while.110 = (s32[]{:T(128)}, f32[4,24,2048]{2,1,0:T(8,128)}, bf16[4,24,2048]{2,1,0:T(8,128)(2,1)S(1)}, s32[]{:T(128)}, s32[]{:T(128)}, /*index=5*/s32[]{:T(128)}, s32[]{:T(128)}) while((s32[]{:T(128)}, f32[4,24,2048]{2,1,0:T(8,128)}, bf16[4,24,2048]{2,1,0:T(8,128)(2,1)S(1)}, s32[]{:T(128)}, s32[]{:T(128)}, ...), condition=%wide.region_32.33_spmd.clone, body=%wide.region_31.32_spmd.clone.sunk | while | flops 221654016 | bytes 1692817 | solution.py:96
  394.9 18.3 %convolution_add_fusion.11 = f32[4,24,2048]{2,1,0:T(8,128)} fusion(f32[2048]{0:T(1024)S(1)} %multiply_subtract_fusion.17, s32[512]{0:T(512)S(1)} %add_select_fusion.25, pred[512]{0:T(512)(128)(4,1)S(1)} %fusion.250, f32[4,24,2048]{2,1,0:T(8,128)} %get-tuple-element.947, pred[]{:T(512)S(6)} %compare.56, ...), kind=kOutput, calls=%fused_computation.130.clone.1 | convolution fusion | flops 221642752 | bytes 1681925 | tf_op jit(solution)/shard_map/while/body/eval_jaxpr/cfj,jm->cfm/dot_general | solution.py:92
  413.2 19.4 %convolution_add_fusion.11 = f32[4,24,2048]{2,1,0:T(8,128)} fusion(f32[2048]{0:T(1024)S(1)} %multiply_subtract_fusion.17, s32[512]{0:T(512)S(1)} %add_select_fusion.25, pred[512]{0:T(512)(128)(4,1)S(1)} %fusion.250, f32[4,24,2048]{2,1,0:T(8,128)} %get-tuple-element.947, pred[]{:T(512)S(6)} %compare.56, ...), kind=kOutput, calls=%fused_computation.130.clone.1 | convolution fusion | flops 221642752 | bytes 1681925 | tf_op jit(solution)/shard_map/while/body/eval_jaxpr/cfj,jm->cfm/dot_general | solution.py:92
  432.7 19.4 %convolution_add_fusion.11 = f32[4,24,2048]{2,1,0:T(8,128)} fusion(f32[2048]{0:T(1024)S(1)} %multiply_subtract_fusion.17, s32[512]{0:T(512)S(1)} %add_select_fusion.25, pred[512]{0:T(512)(128)(4,1)S(1)} %fusion.250, f32[4,24,2048]{2,1,0:T(8,128)} %get-tuple-element.947, pred[]{:T(512)S(6)} %compare.56, ...), kind=kOutput, calls=%fused_computation.130.clone.1 | convolution fusion | flops 221642752 | bytes 1681925 | tf_op jit(solution)/shard_map/while/body/eval_jaxpr/cfj,jm->cfm/dot_general | solution.py:92
  452.2 19.4 %convolution_add_fusion.11 = f32[4,24,2048]{2,1,0:T(8,128)} fusion(f32[2048]{0:T(1024)S(1)} %multiply_subtract_fusion.17, s32[512]{0:T(512)S(1)} %add_select_fusion.25, pred[512]{0:T(512)(128)(4,1)S(1)} %fusion.250, f32[4,24,2048]{2,1,0:T(8,128)} %get-tuple-element.947, pred[]{:T(512)S(6)} %compare.56, ...), kind=kOutput, calls=%fused_computation.130.clone.1 | convolution fusion | flops 221642752 | bytes 1681925 | tf_op jit(solution)/shard_map/while/body/eval_jaxpr/cfj,jm->cfm/dot_general | solution.py:92
  503.8 70.5 %while.111 = (s32[]{:T(128)}, f32[4,2048,24]{1,2,0:T(8,128)S(1)}, bf16[4,24,2048]{2,1,0:T(8,128)(2,1)S(1)}, s32[]{:T(128)}, s32[]{:T(128)}, /*index=5*/s32[]{:T(128)}, s32[]{:T(128)}) while((s32[]{:T(128)}, f32[4,2048,24]{1,2,0:T(8,128)S(1)}, bf16[4,24,2048]{2,1,0:T(8,128)(2,1)S(1)}, s32[]{:T(128)}, s32[]{:T(128)}, ...), condition=%wide.region_34.35_spmd.clone, body=%wide.region_33.34_spmd.clone.sunk | while | flops 221654016 | bytes 1699985 | solution.py:96
  504.2 17.4 %fusion.253 = f32[4,2048,24]{1,2,0:T(8,128)S(1)} fusion(f32[512]{0:T(512)S(1)} %multiply_subtract_fusion.18, s32[512]{0:T(512)S(1)} %iota_add_fusion.15, s32[2048]{0:T(1024)S(1)} %add_select_fusion.26, pred[2048]{0:T(1024)(128)(4,1)S(1)} %iota_compare_fusion.9, f32[4,2048,24]{1,2,0:T(8,128)S(1)} %get-tuple-element.989, pred[]{:T(512)S(6)} %compare.57, ...), kind=kOutput, calls=%fused_computation.160.clone.1 | convolution fusion | flops 221642752 | bytes 1685509 | tf_op jit(solution)/shard_map/while/body/eval_jaxpr/cfm,mk->ckf/dot_general | solution.py:92
  521.7 17.4 %fusion.253 = f32[4,2048,24]{1,2,0:T(8,128)S(1)} fusion(f32[512]{0:T(512)S(1)} %multiply_subtract_fusion.18, s32[512]{0:T(512)S(1)} %iota_add_fusion.15, s32[2048]{0:T(1024)S(1)} %add_select_fusion.26, pred[2048]{0:T(1024)(128)(4,1)S(1)} %iota_compare_fusion.9, f32[4,2048,24]{1,2,0:T(8,128)S(1)} %get-tuple-element.989, pred[]{:T(512)S(6)} %compare.57, ...), kind=kOutput, calls=%fused_computation.160.clone.1 | convolution fusion | flops 221642752 | bytes 1685509 | tf_op jit(solution)/shard_map/while/body/eval_jaxpr/cfm,mk->ckf/dot_general | solution.py:92
  539.2 17.4 %fusion.253 = f32[4,2048,24]{1,2,0:T(8,128)S(1)} fusion(f32[512]{0:T(512)S(1)} %multiply_subtract_fusion.18, s32[512]{0:T(512)S(1)} %iota_add_fusion.15, s32[2048]{0:T(1024)S(1)} %add_select_fusion.26, pred[2048]{0:T(1024)(128)(4,1)S(1)} %iota_compare_fusion.9, f32[4,2048,24]{1,2,0:T(8,128)S(1)} %get-tuple-element.989, pred[]{:T(512)S(6)} %compare.57, ...), kind=kOutput, calls=%fused_computation.160.clone.1 | convolution fusion | flops 221642752 | bytes 1685509 | tf_op jit(solution)/shard_map/while/body/eval_jaxpr/cfm,mk->ckf/dot_general | solution.py:92
  556.7 17.4 %fusion.253 = f32[4,2048,24]{1,2,0:T(8,128)S(1)} fusion(f32[512]{0:T(512)S(1)} %multiply_subtract_fusion.18, s32[512]{0:T(512)S(1)} %iota_add_fusion.15, s32[2048]{0:T(1024)S(1)} %add_select_fusion.26, pred[2048]{0:T(1024)(128)(4,1)S(1)} %iota_compare_fusion.9, f32[4,2048,24]{1,2,0:T(8,128)S(1)} %get-tuple-element.989, pred[]{:T(512)S(6)} %compare.57, ...), kind=kOutput, calls=%fused_computation.160.clone.1 | convolution fusion | flops 221642752 | bytes 1685509 | tf_op jit(solution)/shard_map/while/body/eval_jaxpr/cfm,mk->ckf/dot_general | solution.py:92
  590.3 18.3 %all-to-all-done.2 = bf16[64,2,1536]{2,1,0:T(2,128)(2,1)S(1)} async-done(((bf16[64,2,1536]{2,1,0:T(2,128)(2,1)}), bf16[64,2,1536]{2,1,0:T(2,128)(2,1)S(1)}, u32[]{:S(2)}, u32[]{:S(2)}) %all-to-all-start.2) | async-done | bytes 393248 | tf_op jit(solution)/shard_map/all_to_all | solution.py:233
  (295 shorter events, 289.9 us)
Async XLA Ops:
  0.6 22.5 %copy-start.18 = (s32[4]{0:T(128)S(1)}, s32[4]{0:T(128)}, u32[]{:S(2)}) copy-start(s32[4]{0:T(128)} %param.17) | copy-start | bytes 52
  8.6 33.4 %all-to-all-start = ((bf16[64,2,1536]{2,1,0:T(2,128)(2,1)}), bf16[64,2,1536]{2,1,0:T(2,128)(2,1)S(1)}, u32[]{:S(2)}, u32[]{:S(2)}) async-start(bf16[64,2,1536]{2,1,0:T(2,128)(2,1)} %reshape.510), calls=%async_computation | async-start | bytes 786432 | tf_op jit(solution)/shard_map/all_to_all | solution.py:125
  22.5 229.5 %copy-start.19 = (s32[512]{0:T(512)}, s32[512]{0:T(512)S(1)}, u32[]{:S(2)}) copy-start(s32[512]{0:T(512)S(1)} %add_select_fusion.14) | copy-start | bytes 6148
  23.7 106.2 %copy-start.16 = (s32[4]{0:T(128)}, s32[4]{0:T(128)S(1)}, u32[]{:S(2)}) copy-start(s32[4]{0:T(128)S(1)} %get-tuple-element.753) | copy-start | bytes 52
  47.9 6.5 %copy-start.6 = (f32[4,24,2048]{2,1,0:T(8,128)S(1)}, f32[4,24,2048]{2,1,0:T(8,128)}, u32[]{:S(2)}) copy-start(f32[4,24,2048]{2,1,0:T(8,128)} %custom-call) | copy-start | bytes 2359300
  126.5 3.3 collective-permute-start
  130.1 9.5 %collective-permute-start.1 = (bf16[4,1536]{1,0:T(4,128)(2,1)S(1)}, bf16[4,1536]{1,0:T(4,128)(2,1)S(1)}, u32[]{:S(2)}, u32[]{:S(2)}) collective-permute-start(bf16[4,1536]{1,0:T(4,128)(2,1)S(1)} %slice.297), channel_id=1, source_target_pairs={{1,0},{2,1},{3,2},{4,3},{5,4},{6,5},{7,6},{8,7},{9,8},{10,9},{11,1... | collective-permute-start | bytes 36872 | tf_op jit(solution)/shard_map/ppermute | solution.py:20
  132.6 9.5 %collective-permute-start.2 = (bf16[4,1536]{1,0:T(4,128)(2,1)S(1)}, bf16[4,1536]{1,0:T(4,128)(2,1)S(1)}, u32[]{:S(2)}, u32[]{:S(2)}) collective-permute-start(bf16[4,1536]{1,0:T(4,128)(2,1)S(1)} %slice.303), channel_id=1, source_target_pairs={{1,0},{2,1},{3,2},{4,3},{5,4},{6,5},{7,6},{8,7},{9,8},{10,9},{11,1... | collective-permute-start | bytes 36872 | tf_op jit(solution)/shard_map/ppermute | solution.py:20
  171.5 4.8 copy-start
  176.2 74.6 %copy-start.9 = (bf16[4,96,128]{2,1,0:T(8,128)(2,1)S(1)}, bf16[4,96,128]{2,1,0:T(8,128)(2,1)}, u32[]{:S(2)}) copy-start(bf16[4,96,128]{2,1,0:T(8,128)(2,1)} %get-tuple-element.736) | copy-start | bytes 294916
  176.2 74.6 %copy-start.10 = (bf16[4,96,128]{2,1,0:T(8,128)(2,1)S(1)}, bf16[4,96,128]{2,1,0:T(8,128)(2,1)}, u32[]{:S(2)}) copy-start(bf16[4,96,128]{2,1,0:T(8,128)(2,1)} %get-tuple-element.737) | copy-start | bytes 294916
  176.3 74.6 %copy-start.11 = (bf16[4,96,128]{2,1,0:T(8,128)(2,1)S(1)}, bf16[4,96,128]{2,1,0:T(8,128)(2,1)}, u32[]{:S(2)}) copy-start(bf16[4,96,128]{2,1,0:T(8,128)(2,1)} %get-tuple-element.738) | copy-start | bytes 294916
  176.3 74.6 %copy-start.12 = (bf16[4,96,128]{2,1,0:T(8,128)(2,1)S(1)}, bf16[4,96,128]{2,1,0:T(8,128)(2,1)}, u32[]{:S(2)}) copy-start(bf16[4,96,128]{2,1,0:T(8,128)(2,1)} %get-tuple-element.739) | copy-start | bytes 294916
  252.0 5.4 copy-start.24
  252.0 7.3 %copy-start.28 = (pred[4,48]{1,0:T(4,128)(4,1)S(1)}, pred[4,48]{1,0:T(4,128)(4,1)}, u32[]{:S(2)}) copy-start(pred[4,48]{1,0:T(4,128)(4,1)} %broadcast_compare_fusion.1) | copy-start | bytes 580
  387.0 6.8 %copy-start.15 = (f32[4]{0:T(128)S(1)}, f32[4]{0:T(128)}, u32[]{:S(2)}) copy-start(f32[4]{0:T(128)} %get-tuple-element.751) | copy-start | bytes 52
  480.9 13.6 %slice-start = ((f32[4,51,256]{2,0,1:T(4,128)}), f32[4,48,256]{2,0,1:T(4,128)S(1)}, s32[]{:S(2)}) async-start(f32[4,51,256]{2,0,1:T(4,128)} %pad_add_fusion.2), calls=%async_computation.3 | async-start | bytes 393216 | tf_op jit(solution)/shard_map/slice | solution.py:215
  480.9 13.6 %copy-start.8 = (s32[12288]{0:T(1024)S(1)}, s32[12288]{0:T(1024)}, u32[]{:S(2)}) copy-start(s32[12288]{0:T(1024)} %iota_add_fusion.6) | copy-start | bytes 147460
  480.9 13.6 %copy-start.17 = (s32[4]{0:T(128)S(1)}, s32[4]{0:T(128)}, u32[]{:S(2)}) copy-start(s32[4]{0:T(128)} %copy-done.16) | copy-start | bytes 52
  481.7 22.1 %copy-start.5 = (f32[4,2048,24]{1,2,0:T(8,128)S(1)}, f32[4,2048,24]{1,2,0:T(8,128)}, u32[]{:S(2)}) copy-start(f32[4,2048,24]{1,2,0:T(8,128)} %custom-call.5) | copy-start | bytes 2359300
  482.2 12.3 %collective-permute-start.3 = (f32[4,1536]{1,0:T(4,128)S(1)}, f32[4,1536]{1,0:T(4,128)S(1)}, u32[]{:S(2)}, u32[]{:S(2)}) collective-permute-start(f32[4,1536]{1,0:T(4,128)S(1)} %add_add_fusion.3), channel_id=1, source_target_pairs={{0,1},{1,2},{2,3},{3,4},{4,5},{5,6},{6,7},{7,8},{8,9},{9,10},{10,1... | collective-permute-start | bytes 73736 | tf_op jit(solution)/shard_map/ppermute | solution.py:20
  491.3 88.7 %all-to-all-start.1 = ((f32[4,1,1]{2,1,0:T(1,128)}), f32[4,1,1]{2,1,0:T(1,128)S(1)}, u32[]{:S(2)}, u32[]{:S(2)}) async-start(f32[4,1,1]{2,1,0:T(1,128)} %broadcast_in_dim.314), calls=%async_computation.1 | async-start | bytes 4096 | tf_op jit(solution)/shard_map/all_to_all | solution.py:31
  494.7 9.0 %collective-permute-start.4 = (bf16[4,3,512]{2,1,0:T(4,128)(2,1)S(1)}, bf16[4,3,512]{2,1,0:T(4,128)(2,1)S(1)}, u32[]{:S(2)}, u32[]{:S(2)}) collective-permute-start(bf16[4,3,512]{2,1,0:T(4,128)(2,1)S(1)} %slice.346), channel_id=1, source_target_pairs={{1,0},{2,1},{3,2},{4,3},{5,4},{6,5},{7,6},{8,7},{9,8},{10,9},{11,1... | collective-permute-start | bytes 36872 | tf_op jit(solution)/shard_map/ppermute | solution.py:20
  580.0 28.6 %all-to-all-start.2 = ((bf16[64,2,1536]{2,1,0:T(2,128)(2,1)}), bf16[64,2,1536]{2,1,0:T(2,128)(2,1)S(1)}, u32[]{:S(2)}, u32[]{:S(2)}) async-start(bf16[64,2,1536]{2,1,0:T(2,128)(2,1)} %reshape.512), calls=%async_computation.2 | async-start | bytes 786432 | tf_op jit(solution)/shard_map/all_to_all | solution.py:233
  (15 other events, 48.0 us)
